TPU v7x, 256 devices: a whole 4x4x8 slice. The times are simulated.
256 devices in a mesh: dp: 16 (over z, y_lo), ctx: 16 (over x, y_hi, core).
Axes of the slice: x: 4, y: 4 (y_hi: 2, y_lo: 2; y = y_hi * 2 + y_lo), z: 8, core: 2. Of those that a mesh axis runs over, the one named last changes fastest.
Arguments:
- queries: bfloat16 [65536, 2048], P(('dp', 'ctx')), parts along dimension 0, may hold values from -100 to 100
- keys: bfloat16 [65536, 2048], P(('dp', 'ctx')), parts along dimension 0, may hold values from -5 to 5
- values: bfloat16 [65536, 2048], P(('dp', 'ctx')), parts along dimension 0, may hold values from -6 to 6
- outputs: bfloat16 [65536, 2048], P(('dp', 'ctx')), parts along dimension 0, may hold values from -6 to 6
- out_grad: bfloat16 [65536, 2048], P(('dp', 'ctx')), parts along dimension 0, may hold values from -6 to 6
- segment_ids: int32 [65536], P(('dp', 'ctx')), parts along dimension 0, may hold values from 0 to 7, never falling along the last dimension, each value on 1 to 1536 neighbouring positions
Outputs:
- query_grad: bfloat16 [65536, 2048], P(('dp', 'ctx')), parts along dimension 0
- key_grad: bfloat16 [65536, 2048], P(('dp', 'ctx')), parts along dimension 0
- value_grad: bfloat16 [65536, 2048], P(('dp', 'ctx')), parts along dimension 0
There are 16 independent parts, one for each index of `dp`. A program takes and returns all parts, laid end to end along the dimension named above; each array names one. Nothing has to cross between parts.
Inputs may be any that keep to these rules, and one draw needn't show every extreme that they name: `segment_ids`: ids never fall; each document holds 1 to 1536 positions, one exactly that many.
All inputs are finite; a program needn't handle non-finite values.
Results may differ from a plain program's by a relative error of at most 0.0049.
Values may be sent and summed in bfloat16 or wider, within the bound.
A program may use at most 128 MiB of HBM per device.

v0:
```python
import jax
import jax.numpy as jnp
from jax import lax
from jax.experimental import pallas as pl
from jax.experimental.pallas import tpu as pltpu
from jax.sharding import PartitionSpec as P

HEAD = 128
WIN = 4
WINDOW = 768
GROUP = 4
LOG2E = 1.4426950408889634
masked_score = -1e30
MESH = pl.DeviceIdType.MESH


def dot(a, b, dims):
    return lax.dot_general(a, b, (dims, ((), ())), preferred_element_type=jnp.float32)


def kernel(
    q_hbm, k_hbm, v_hbm, o_hbm, do_hbm, seg_hbm,
    dq_hbm, dk_hbm, dv_hbm,
    qb, dob, kb, vb, ob, dol, seg_row, segsrc, segs, dsrc, deltas, lows,
    dk_acc, dv_acc, dq_out, dk_out, dv_out, halo_out, halo_in,
    in_send, in_recv, fwd_send, fwd_recv, ret_send, ret_recv, out_send, out_recv,
    seg_send, seg_recv, del_send, del_recv, loc_sem,
):
    rows = q_hbm.shape[0]
    heads = q_hbm.shape[1] // HEAD
    mine = heads // GROUP
    halo = (WIN - 1) * rows
    span = WIN * rows
    scale = HEAD ** (-0.5)
    n_ctx = lax.axis_size("ctx")
    n_x = n_ctx // GROUP
    me = lax.axis_index("ctx")
    x = me // GROUP
    g = lax.rem(me, GROUP)
    y = g // 2
    c = lax.rem(g, 2)
    peers = [2 * (1 - y) + c, 2 * (1 - y) + (1 - c), 2 * y + (1 - c)]
    ahead = lax.rem(x + 1, n_x) * GROUP + g
    behind = lax.rem(x + n_x - 1, n_x) * GROUP + g

    o_copy = pltpu.make_async_copy(o_hbm, ob, loc_sem.at[0])
    do_copy = pltpu.make_async_copy(do_hbm, dol, loc_sem.at[1])
    seg_copy = pltpu.make_async_copy(seg_hbm, seg_row, loc_sem.at[2])
    seg_copy.start()
    o_copy.start()
    do_copy.start()

    barrier = pltpu.get_barrier_semaphore()
    for other in [x * GROUP + p for p in peers] + [ahead, behind]:
        pl.semaphore_signal(barrier, inc=1, device_id={"ctx": other}, device_id_type=MESH)
    pl.semaphore_wait(barrier, 5)

    def remote(src, dst, send, recv, to):
        return pltpu.make_async_remote_copy(
            src_ref=src, dst_ref=dst, send_sem=send, recv_sem=recv,
            device_id={"ctx": to}, device_id_type=MESH,
        )

    def wait_bytes(ref, sem):
        pltpu.make_async_copy(ref, ref, sem).wait()

    def columns(owner, j):
        return pl.ds(pl.multiple_of((owner * mine + j) * HEAD, HEAD), HEAD)

    def place(block, first):
        return pl.ds(pl.multiple_of(first + block * rows, rows), rows)

    arrays = [(k_hbm, kb, halo), (v_hbm, vb, halo), (q_hbm, qb, 0), (do_hbm, dob, 0)]

    seg_copy.wait()
    segsrc[...] = jnp.broadcast_to(seg_row[...], segsrc.shape)
    segs[WIN - 1 + g] = segsrc[...]
    for p in peers:
        remote(segsrc, segs.at[WIN - 1 + g], seg_send.at[0], seg_recv.at[0], x * GROUP + p).start()

    def start_in(j, stage):
        for a in range(2 * stage, 2 * stage + 2):
            src, dst, first = arrays[a]
            for p in peers:
                remote(
                    src.at[:, columns(p, j)], dst.at[j, place(g, first)],
                    in_send.at[j, a], in_recv.at[j, a], x * GROUP + p,
                ).start()
            pltpu.make_async_copy(
                src.at[:, columns(g, j)], dst.at[j, place(g, first)], in_recv.at[j, a]
            ).start()

    def wait_in(j, stage):
        for a in range(2 * stage, 2 * stage + 2):
            _, dst, first = arrays[a]
            wait_bytes(dst.at[j, first:], in_recv.at[j, a])
            wait_bytes(dst.at[j, 0 : (GROUP - 1) * rows], in_send.at[j, a])

    start_in(0, 0)
    start_in(0, 1)

    o_copy.wait()
    do_copy.wait()

    def one_delta(h, carry):
        cols = pl.ds(pl.multiple_of(h * HEAD, HEAD), HEAD)
        product = ob[:, cols].astype(jnp.float32) * dol[:, cols].astype(jnp.float32)
        dsrc[h // mine, pl.ds(lax.rem(h, mine), 1), :] = jnp.sum(product.T, axis=0, keepdims=True)
        return carry

    lax.fori_loop(0, heads, one_delta, 0)
    deltas[g] = dsrc[g]
    for p in peers:
        remote(dsrc.at[p], deltas.at[g], del_send.at[0], del_recv.at[0], x * GROUP + p).start()

    wait_bytes(segs.at[0 : GROUP - 1], seg_recv.at[0])
    seg_fwd = remote(segs.at[WIN:], segs.at[0 : WIN - 1], seg_send.at[1], seg_recv.at[1], ahead)
    seg_fwd.start()
    seg_fwd.wait_recv()
    seg_fwd.wait_send()
    for b in range(GROUP):
        ids = segs[WIN - 1 + b][0:1, :]
        low = lax.broadcasted_iota(jnp.int32, (1, rows), 1) + (span - rows - WINDOW + 1)
        first = jnp.zeros((1, rows), jnp.int32)
        for w in range(b, b + WIN):
            theirs = segs[w][0:1, :]
            if w < WIN - 1:
                theirs = jnp.where(x == 0, -1, theirs)
            for doc in range(8):
                fewer = jnp.sum((theirs < doc).astype(jnp.int32), axis=1, keepdims=True)
                first = first + jnp.where(ids == doc, fewer, 0)
        lows[b] = jnp.broadcast_to(jnp.maximum(low, first), (8, rows))

    def compute(j):
        dk_acc[j] = jnp.zeros(dk_acc.shape[1:], jnp.float32)
        dv_acc[j] = jnp.zeros(dv_acc.shape[1:], jnp.float32)

        def block(b, carry):
            window = pl.ds(pl.multiple_of(b * rows, rows), span)
            own = pl.ds(pl.multiple_of(b * rows, rows), rows)
            query, grad = qb[j, own, :], dob[j, own, :]
            key, value = kb[j, window, :], vb[j, window, :]
            place_k = lax.broadcasted_iota(jnp.int32, (span, rows), 0)
            place_q = lax.broadcasted_iota(jnp.int32, (span, rows), 1) + halo
            visible = (place_k <= place_q) & (place_k >= lows[b][0:1, :])
            scores = dot(key, query, ((1,), (1,))) * (scale * LOG2E)
            scores = jnp.where(visible, scores, masked_score)
            top = jnp.max(scores, axis=0, keepdims=True)
            weights = jnp.exp2(scores - top)
            total = jnp.sum(weights, axis=0, keepdims=True)
            probs = weights * (1.0 / total)
            probs_low = probs.astype(jnp.bfloat16)
            dv_acc[j, window, :] += dot(probs_low, grad, ((1,), (0,)))
            dprobs = dot(value, grad, ((1,), (1,)))
            delta = deltas[b, pl.ds(j, 1), :]
            dscores = (probs * (dprobs - delta)).astype(jnp.bfloat16)
            dk_acc[j, window, :] += dot(dscores, query, ((1,), (0,)))
            dq_out[j, own, :] = (dot(dscores, key, ((0,), (0,))) * scale).astype(jnp.bfloat16)
            return carry

        lax.fori_loop(0, GROUP, block, 0)

    def send_out(j, a, src, dst):
        for p in peers:
            remote(
                src.at[j, place(p, 0)], dst.at[:, columns(g, j)],
                out_send.at[j, a], out_recv.at[j, a], x * GROUP + p,
            ).start()
        pltpu.make_async_copy(
            src.at[j, place(g, 0)], dst.at[:, columns(g, j)], out_recv.at[j, a]
        ).start()

    def forward(j, a, buf):
        return remote(
            buf.at[j, span : span + halo], buf.at[j, 0:halo],
            fwd_send.at[j, a], fwd_recv.at[j, a], ahead,
        )

    def give_back(j, a):
        return remote(
            halo_out.at[a, j], halo_in.at[a, j], ret_send.at[j, a], ret_recv.at[j, a], behind
        )

    def finish(j):
        for a, (acc, out, factor) in enumerate(((dk_acc, dk_out, scale), (dv_acc, dv_out, 1.0))):
            give_back(j, a).wait_recv()
            out[j, 0:rows, :] = (acc[j, halo:span, :] * factor).astype(jnp.bfloat16)
            out[j, rows:, :] = (
                acc[j, span:, :] * factor + halo_in[a, j].astype(jnp.float32)
            ).astype(jnp.bfloat16)

    def send_key_value(j):
        send_out(j, 1, dk_out, dk_hbm)
        send_out(j, 2, dv_out, dv_hbm)

    last = mine - 1

    def step(t, carry):
        @pl.when(t < mine)
        def _():
            wait_in(t, 0)
            for a, buf in enumerate((kb, vb)):
                forward(t, a, buf).start()

        @pl.when(t < last)
        def _():
            start_in(t + 1, 0)

        @pl.when(t == last)
        def _():
            def late(j, carry):
                send_out(j, 0, dq_out, dq_hbm)
                return carry

            lax.fori_loop(0, last - 1, late, 0)

        @pl.when((t >= 1) & (t <= mine))
        def _():
            j = t - 1

            @pl.when(j == 0)
            def _():
                wait_bytes(deltas.at[0 : GROUP - 1], del_recv.at[0])

            for a, buf in enumerate((kb, vb)):
                forward(j, a, buf).wait_recv()
            compute(j)
            halo_out[0, j] = (dk_acc[j, 0:halo, :] * scale).astype(jnp.bfloat16)
            halo_out[1, j] = dv_acc[j, 0:halo, :].astype(jnp.bfloat16)
            for a in range(2):
                give_back(j, a).start()

            @pl.when(t >= last)
            def _():
                send_out(j, 0, dq_out, dq_hbm)

        @pl.when(t < mine)
        def _():
            wait_in(t, 1)

        @pl.when(t < last)
        def _():
            start_in(t + 1, 1)

        @pl.when(t >= 2)
        def _():
            finish(t - 2)

        @pl.when(t == last)
        def _():
            def late(j, carry):
                send_key_value(j)
                return carry

            lax.fori_loop(0, last - 2, late, 0)

        @pl.when(t >= last)
        def _():
            send_key_value(t - 2)

        return carry

    lax.fori_loop(0, mine + 2, step, 0)

    wait_bytes(segs.at[0 : GROUP - 1], seg_send.at[0])
    wait_bytes(deltas.at[0 : GROUP - 1], del_send.at[0])

    def drain(j, carry):
        for a, buf in enumerate((kb, vb)):
            forward(j, a, buf).wait_send()
            give_back(j, a).wait_send()
        for a in range(3):
            wait_bytes(dq_out.at[j, 0 : (GROUP - 1) * rows], out_send.at[j, a])
            wait_bytes(dq_out.at[j], out_recv.at[j, a])
        return carry

    lax.fori_loop(0, mine, drain, 0)


def body(queries, keys, values, outputs, out_grad, segment_ids):
    rows, width = queries.shape
    mine = width // HEAD // GROUP
    halo, group = (WIN - 1) * rows, GROUP * rows
    bf16, f32, i32 = jnp.bfloat16, jnp.float32, jnp.int32
    dma = pltpu.SemaphoreType.DMA
    anywhere = pl.BlockSpec(memory_space=pltpu.HBM)
    return pl.pallas_call(
        kernel,
        out_shape=[jax.ShapeDtypeStruct((rows, width), bf16)] * 3,
        in_specs=[anywhere] * 6,
        out_specs=[anywhere] * 3,
        scratch_shapes=[
            pltpu.VMEM((mine, group, HEAD), bf16),
            pltpu.VMEM((mine, group, HEAD), bf16),
            pltpu.VMEM((mine, halo + group, HEAD), bf16),
            pltpu.VMEM((mine, halo + group, HEAD), bf16),
            pltpu.VMEM((rows, width), bf16),
            pltpu.VMEM((rows, width), bf16),
            pltpu.VMEM((1, rows), i32),
            pltpu.VMEM((8, rows), i32),
            pltpu.VMEM((WIN - 1 + GROUP, 8, rows), i32),
            pltpu.VMEM((GROUP, 8, rows), f32),
            pltpu.VMEM((GROUP, 8, rows), f32),
            pltpu.VMEM((GROUP, 8, rows), i32),
            pltpu.VMEM((mine, halo + group, HEAD), f32),
            pltpu.VMEM((mine, halo + group, HEAD), f32),
            pltpu.VMEM((mine, group, HEAD), bf16),
            pltpu.VMEM((mine, group, HEAD), bf16),
            pltpu.VMEM((mine, group, HEAD), bf16),
            pltpu.VMEM((2, mine, halo, HEAD), bf16),
            pltpu.VMEM((2, mine, halo, HEAD), bf16),
            dma((mine, 4)), dma((mine, 4)),
            dma((mine, 2)), dma((mine, 2)),
            dma((mine, 2)), dma((mine, 2)),
            dma((mine, 3)), dma((mine, 3)),
            dma((2,)), dma((2,)),
            dma((1,)), dma((1,)),
            dma((3,)),
        ],
        compiler_params=pltpu.CompilerParams(
            collective_id=0, has_side_effects=True, vmem_limit_bytes=50 * 1024 * 1024
        ),
        name="window_attention_grads",
    )(queries, keys, values, outputs, out_grad, segment_ids.reshape(1, rows))


def solution(mesh):
    part = P(("dp", "ctx"), None)
    return jax.shard_map(
        body,
        mesh=mesh,
        in_specs=(part, part, part, part, part, P(("dp", "ctx"))),
        out_specs=(part, part, part),
        check_vma=False,
    )
```

profile of v0, /device:TPU:1, one launch (start us, length us, event | category | flops | bytes accessed | tf_op | source)
XLA Modules:
  0.0 91.7 jit_solution(15382085345695338995)
XLA Ops:
  0.6 0.0 copy-start
  0.6 0.7 copy-done
  1.3 87.4 %window_attention_grads.1 = (bf16[256,2048]{1,0:T(8,128)(2,1)S(1)}, bf16[256,2048]{1,0:T(8,128)(2,1)S(1)}, bf16[256,2048]{1,0:T(8,128)(2,1)S(1)}) custom-call(bf16[256,2048]{1,0:T(8,128)(2,1)} %q_hbm.1, bf16[256,2048]{1,0:T(8,128)(2,1)} %k_hbm.1, bf16[256,2048]{1,0:T(8,128)(2,1)} %v_hbm.1, bf16[256,2048]{1,0:T(8,128)(2,1)} %o_hbm.1, ...), custom_call_target="tpu_custom_call" | custom-call | tf_op jit(solution)/shard_map/window_attention_grads/pallas_call | solution.py:287
  88.7 1.0 %copy.12 = bf16[256,2048]{1,0:T(8,128)(2,1)} copy(bf16[256,2048]{1,0:T(8,128)(2,1)S(1)} %get-tuple-element.6) | data formatting | bytes 2097152
  89.7 1.0 %copy.13 = bf16[256,2048]{1,0:T(8,128)(2,1)} copy(bf16[256,2048]{1,0:T(8,128)(2,1)S(1)} %get-tuple-element.7) | data formatting | bytes 2097152
  90.7 1.0 %copy.14 = bf16[256,2048]{1,0:T(8,128)(2,1)} copy(bf16[256,2048]{1,0:T(8,128)(2,1)S(1)} %get-tuple-element.8) | data formatting | bytes 2097152
Async XLA Ops:
  0.6 0.7 copy-start
where the time goes:
time: 91.8 us; the launch traced here: 91.7 us
  Pallas kernels  87.4 us (95%)
  local copies, waits for them, and re-layouts  3.58 us (4%)
    pallas_call x1, Pallas kernels, body(): pl.pallas_call(kernel, out_shape=[jax.ShapeDtypeStruct((rows, width), bf1...  87.4 us
    unnamed x5, local copies, waits for them, and re-layouts  3.58 us

commit v1 on v0

--- a/solution.py
+++ b/solution.py
@@ -21,7 +21,7 @@
 def kernel(
     q_hbm, k_hbm, v_hbm, o_hbm, do_hbm, seg_hbm,
     dq_hbm, dk_hbm, dv_hbm,
-    qb, dob, kb, vb, ob, dol, seg_row, segsrc, segs, dsrc, deltas, lows,
+    qb, dob, kb, vb, ob, dol, seg_row, segs, dsrc, deltas, lows,
     dk_acc, dv_acc, dq_out, dk_out, dv_out, halo_out, halo_in,
     in_send, in_recv, fwd_send, fwd_recv, ret_send, ret_recv, out_send, out_recv,
     seg_send, seg_recv, del_send, del_recv, loc_sem,
@@ -32,6 +32,7 @@
     halo = (WIN - 1) * rows
     span = WIN * rows
     scale = HEAD ** (-0.5)
+    twice = 2.0 * scale
     n_ctx = lax.axis_size("ctx")
     n_x = n_ctx // GROUP
     me = lax.axis_index("ctx")
@@ -73,10 +74,9 @@
     arrays = [(k_hbm, kb, halo), (v_hbm, vb, halo), (q_hbm, qb, 0), (do_hbm, dob, 0)]
 
     seg_copy.wait()
-    segsrc[...] = jnp.broadcast_to(seg_row[...], segsrc.shape)
-    segs[WIN - 1 + g] = segsrc[...]
+    segs[WIN - 1 + g] = seg_row[...]
     for p in peers:
-        remote(segsrc, segs.at[WIN - 1 + g], seg_send.at[0], seg_recv.at[0], x * GROUP + p).start()
+        remote(seg_row, segs.at[WIN - 1 + g], seg_send.at[0], seg_recv.at[0], x * GROUP + p).start()
 
     def start_in(j, stage):
         for a in range(2 * stage, 2 * stage + 2):
@@ -155,7 +155,7 @@
             delta = deltas[b, pl.ds(j, 1), :]
             dscores = (probs * (dprobs - delta)).astype(jnp.bfloat16)
             dk_acc[j, window, :] += dot(dscores, query, ((1,), (0,)))
-            dq_out[j, own, :] = (dot(dscores, key, ((0,), (0,))) * scale).astype(jnp.bfloat16)
+            dq_out[j, own, :] = (dot(dscores, key, ((0,), (0,))) * twice).astype(jnp.bfloat16)
             return carry
 
         lax.fori_loop(0, GROUP, block, 0)
@@ -182,7 +182,7 @@
         )
 
     def finish(j):
-        for a, (acc, out, factor) in enumerate(((dk_acc, dk_out, scale), (dv_acc, dv_out, 1.0))):
+        for a, (acc, out, factor) in enumerate(((dk_acc, dk_out, twice), (dv_acc, dv_out, 2.0))):
             give_back(j, a).wait_recv()
             out[j, 0:rows, :] = (acc[j, halo:span, :] * factor).astype(jnp.bfloat16)
             out[j, rows:, :] = (
@@ -225,8 +225,8 @@
             for a, buf in enumerate((kb, vb)):
                 forward(j, a, buf).wait_recv()
             compute(j)
-            halo_out[0, j] = (dk_acc[j, 0:halo, :] * scale).astype(jnp.bfloat16)
-            halo_out[1, j] = dv_acc[j, 0:halo, :].astype(jnp.bfloat16)
+            halo_out[0, j] = (dk_acc[j, 0:halo, :] * twice).astype(jnp.bfloat16)
+            halo_out[1, j] = (dv_acc[j, 0:halo, :] * 2.0).astype(jnp.bfloat16)
             for a in range(2):
                 give_back(j, a).start()
 
@@ -284,7 +284,7 @@
     bf16, f32, i32 = jnp.bfloat16, jnp.float32, jnp.int32
     dma = pltpu.SemaphoreType.DMA
     anywhere = pl.BlockSpec(memory_space=pltpu.HBM)
-    return pl.pallas_call(
+    doubled = pl.pallas_call(
         kernel,
         out_shape=[jax.ShapeDtypeStruct((rows, width), bf16)] * 3,
         in_specs=[anywhere] * 6,
@@ -297,10 +297,9 @@
             pltpu.VMEM((rows, width), bf16),
             pltpu.VMEM((rows, width), bf16),
             pltpu.VMEM((1, rows), i32),
-            pltpu.VMEM((8, rows), i32),
-            pltpu.VMEM((WIN - 1 + GROUP, 8, rows), i32),
-            pltpu.VMEM((GROUP, 8, rows), f32),
-            pltpu.VMEM((GROUP, 8, rows), f32),
+            pltpu.VMEM((WIN - 1 + GROUP, 1, rows), i32),
+            pltpu.VMEM((GROUP, mine, rows), f32),
+            pltpu.VMEM((GROUP, mine, rows), f32),
             pltpu.VMEM((GROUP, 8, rows), i32),
             pltpu.VMEM((mine, halo + group, HEAD), f32),
             pltpu.VMEM((mine, halo + group, HEAD), f32),
@@ -322,6 +321,7 @@
         ),
         name="window_attention_grads",
     )(queries, keys, values, outputs, out_grad, segment_ids.reshape(1, rows))
+    return tuple(grad * 0.5 for grad in doubled)
 
 
 def solution(mesh):

time: 91.8 us -> 91.1 us (level)
  local copies, waits for them, and re-layouts: 3.58 us -> 0.67 us
  other arithmetic: 0 us -> 2.56 us
    unnamed x5 -> x2, local copies, waits for them, and re-layouts: 3.58 us -> 0.67 us
    mul x0 -> x2, other arithmetic: none -> 2.56 us  [body(): return tuple((grad * 0.5 for grad in doubled))]
where the time goes in v1:
time: 91.1 us; the launch traced here: 91 us
  Pallas kernels  87.1 us (96%)
  other arithmetic  2.56 us (3%)
    pallas_call x1, Pallas kernels, body(): pl.pallas_call(kernel, out_shape=[jax.ShapeDtypeStruct((rows, width), bf1...  87.1 us
    mul x2, other arithmetic, body(): return tuple((grad * 0.5 for grad in doubled))  2.56 us

profile of v1, /device:TPU:1, one launch (start us, length us, event | category | flops | bytes accessed | tf_op | source)
XLA Modules:
  0.0 91.0 jit_solution(16999365179960104151)
XLA Ops:
  0.6 0.0 copy-start
  0.6 0.7 copy-done
  1.3 87.1 %window_attention_grads.1 = (bf16[256,2048]{1,0:T(8,128)(2,1)S(1)}, bf16[256,2048]{1,0:T(8,128)(2,1)S(1)}, bf16[256,2048]{1,0:T(8,128)(2,1)S(1)}) custom-call(bf16[256,2048]{1,0:T(8,128)(2,1)} %q_hbm.1, bf16[256,2048]{1,0:T(8,128)(2,1)} %k_hbm.1, bf16[256,2048]{1,0:T(8,128)(2,1)} %v_hbm.1, bf16[256,2048]{1,0:T(8,128)(2,1)} %o_hbm.1, ...), custom_call_target="tpu_custom_call" | custom-call | tf_op jit(solution)/shard_map/window_attention_grads/pallas_call | solution.py:287
  88.4 1.1 %broadcast_multiply_fusion.2 = bf16[256,2048]{1,0:T(8,128)(2,1)} fusion(bf16[256,2048]{1,0:T(8,128)(2,1)S(1)} %get-tuple-element.6), kind=kLoop, calls=%fused_computation.2 | loop fusion | flops 524288 | bytes 2097152 | tf_op jit(solution)/shard_map/mul | solution.py:324
  89.5 1.5 %broadcast_multiply_fusion = (bf16[256,2048]{1,0:T(8,128)(2,1)}, bf16[256,2048]{1,0:T(8,128)(2,1)}) fusion(bf16[256,2048]{1,0:T(8,128)(2,1)S(1)} %get-tuple-element.8, bf16[256,2048]{1,0:T(8,128)(2,1)S(1)} %get-tuple-element.7), kind=kLoop, calls=%fused_computation | loop fusion | flops 1048576 | bytes 4194304 | tf_op jit(solution)/shard_map/mul | solution.py:324
Async XLA Ops:
  0.6 0.7 copy-start

commit v2 on v1

--- a/solution.py
+++ b/solution.py
@@ -9,6 +9,7 @@
 WIN = 4
 WINDOW = 768
 GROUP = 4
+DEPTH = 3
 LOG2E = 1.4426950408889634
 masked_score = -1e30
 MESH = pl.DeviceIdType.MESH
@@ -73,11 +74,6 @@
 
     arrays = [(k_hbm, kb, halo), (v_hbm, vb, halo), (q_hbm, qb, 0), (do_hbm, dob, 0)]
 
-    seg_copy.wait()
-    segs[WIN - 1 + g] = seg_row[...]
-    for p in peers:
-        remote(seg_row, segs.at[WIN - 1 + g], seg_send.at[0], seg_recv.at[0], x * GROUP + p).start()
-
     def start_in(j, stage):
         for a in range(2 * stage, 2 * stage + 2):
             src, dst, first = arrays[a]
@@ -90,6 +86,13 @@
                 src.at[:, columns(g, j)], dst.at[j, place(g, first)], in_recv.at[j, a]
             ).start()
 
+    def start_ahead(j, stage):
+        later, kind = j + (stage + DEPTH) // 2, (stage + DEPTH) % 2
+
+        @pl.when(later < mine)
+        def _():
+            start_in(later, kind)
+
     def wait_in(j, stage):
         for a in range(2 * stage, 2 * stage + 2):
             _, dst, first = arrays[a]
@@ -97,7 +100,14 @@
             wait_bytes(dst.at[j, 0 : (GROUP - 1) * rows], in_send.at[j, a])
 
     start_in(0, 0)
-    start_in(0, 1)
+
+    seg_copy.wait()
+    segs[WIN - 1 + g] = seg_row[...]
+    for p in peers:
+        remote(seg_row, segs.at[WIN - 1 + g], seg_send.at[0], seg_recv.at[0], x * GROUP + p).start()
+
+    for stage in range(1, DEPTH):
+        start_in(stage // 2, stage % 2)
 
     o_copy.wait()
     do_copy.wait()
@@ -202,9 +212,7 @@
             for a, buf in enumerate((kb, vb)):
                 forward(t, a, buf).start()
 
-        @pl.when(t < last)
-        def _():
-            start_in(t + 1, 0)
+        start_ahead(t, 0)
 
         @pl.when(t == last)
         def _():
@@ -238,9 +246,7 @@
         def _():
             wait_in(t, 1)
 
-        @pl.when(t < last)
-        def _():
-            start_in(t + 1, 1)
+        start_ahead(t, 1)
 
         @pl.when(t >= 2)
         def _():

time: 91.1 us -> 91.1 us (level)
  no operation moved by 1% of the time
where the time goes in v2:
time: 91.1 us; the launch traced here: 91 us
  Pallas kernels  87.1 us (96%)
  other arithmetic  2.56 us (3%)
    pallas_call x1, Pallas kernels, body(): pl.pallas_call(kernel, out_shape=[jax.ShapeDtypeStruct((rows, width), bf1...  87.1 us
    mul x2, other arithmetic, body(): return tuple((grad * 0.5 for grad in doubled))  2.56 us

profile of v2, /device:TPU:1, one launch (start us, length us, event | category | flops | bytes accessed | tf_op | source)
XLA Modules:
  0.0 91.0 jit_solution(5970147719749335417)
XLA Ops:
  0.6 0.0 copy-start
  0.6 0.7 copy-done
  1.3 87.1 %window_attention_grads.1 = (bf16[256,2048]{1,0:T(8,128)(2,1)S(1)}, bf16[256,2048]{1,0:T(8,128)(2,1)S(1)}, bf16[256,2048]{1,0:T(8,128)(2,1)S(1)}) custom-call(bf16[256,2048]{1,0:T(8,128)(2,1)} %q_hbm.1, bf16[256,2048]{1,0:T(8,128)(2,1)} %k_hbm.1, bf16[256,2048]{1,0:T(8,128)(2,1)} %v_hbm.1, bf16[256,2048]{1,0:T(8,128)(2,1)} %o_hbm.1, ...), custom_call_target="tpu_custom_call" | custom-call | tf_op jit(solution)/shard_map/window_attention_grads/pallas_call | solution.py:293
  88.4 1.1 %broadcast_multiply_fusion.2 = bf16[256,2048]{1,0:T(8,128)(2,1)} fusion(bf16[256,2048]{1,0:T(8,128)(2,1)S(1)} %get-tuple-element.6), kind=kLoop, calls=%fused_computation.2 | loop fusion | flops 524288 | bytes 2097152 | tf_op jit(solution)/shard_map/mul | solution.py:330
  89.5 1.5 %broadcast_multiply_fusion = (bf16[256,2048]{1,0:T(8,128)(2,1)}, bf16[256,2048]{1,0:T(8,128)(2,1)}) fusion(bf16[256,2048]{1,0:T(8,128)(2,1)S(1)} %get-tuple-element.8, bf16[256,2048]{1,0:T(8,128)(2,1)S(1)} %get-tuple-element.7), kind=kLoop, calls=%fused_computation | loop fusion | flops 1048576 | bytes 4194304 | tf_op jit(solution)/shard_map/mul | solution.py:330
Async XLA Ops:
  0.6 0.7 copy-start

commit v3 on v1

--- a/solution.py
+++ b/solution.py
@@ -48,8 +48,6 @@
     do_copy = pltpu.make_async_copy(do_hbm, dol, loc_sem.at[1])
     seg_copy = pltpu.make_async_copy(seg_hbm, seg_row, loc_sem.at[2])
     seg_copy.start()
-    o_copy.start()
-    do_copy.start()
 
     barrier = pltpu.get_barrier_semaphore()
     for other in [x * GROUP + p for p in peers] + [ahead, behind]:
@@ -98,6 +96,9 @@
 
     start_in(0, 0)
     start_in(0, 1)
+
+    o_copy.start()
+    do_copy.start()
 
     o_copy.wait()
     do_copy.wait()

time: 91.1 us -> 91.1 us (level)
  no operation moved by 1% of the time
where the time goes in v3:
time: 91.1 us; the launch traced here: 91 us
  Pallas kernels  87.1 us (96%)
  other arithmetic  2.56 us (3%)
    pallas_call x1, Pallas kernels, body(): pl.pallas_call(kernel, out_shape=[jax.ShapeDtypeStruct((rows, width), bf1...  87.1 us
    mul x2, other arithmetic, body(): return tuple((grad * 0.5 for grad in doubled))  2.56 us

profile of v3, /device:TPU:1, one launch (start us, length us, event | category | flops | bytes accessed | tf_op | source)
XLA Modules:
  0.0 91.0 jit_solution(15723718766232629827)
XLA Ops:
  0.6 0.0 copy-start
  0.6 0.7 copy-done
  1.3 87.1 %window_attention_grads.1 = (bf16[256,2048]{1,0:T(8,128)(2,1)S(1)}, bf16[256,2048]{1,0:T(8,128)(2,1)S(1)}, bf16[256,2048]{1,0:T(8,128)(2,1)S(1)}) custom-call(bf16[256,2048]{1,0:T(8,128)(2,1)} %q_hbm.1, bf16[256,2048]{1,0:T(8,128)(2,1)} %k_hbm.1, bf16[256,2048]{1,0:T(8,128)(2,1)} %v_hbm.1, bf16[256,2048]{1,0:T(8,128)(2,1)} %o_hbm.1, ...), custom_call_target="tpu_custom_call" | custom-call | tf_op jit(solution)/shard_map/window_attention_grads/pallas_call | solution.py:288
  88.4 1.1 %broadcast_multiply_fusion.2 = bf16[256,2048]{1,0:T(8,128)(2,1)} fusion(bf16[256,2048]{1,0:T(8,128)(2,1)S(1)} %get-tuple-element.6), kind=kLoop, calls=%fused_computation.2 | loop fusion | flops 524288 | bytes 2097152 | tf_op jit(solution)/shard_map/mul | solution.py:325
  89.5 1.5 %broadcast_multiply_fusion = (bf16[256,2048]{1,0:T(8,128)(2,1)}, bf16[256,2048]{1,0:T(8,128)(2,1)}) fusion(bf16[256,2048]{1,0:T(8,128)(2,1)S(1)} %get-tuple-element.8, bf16[256,2048]{1,0:T(8,128)(2,1)S(1)} %get-tuple-element.7), kind=kLoop, calls=%fused_computation | loop fusion | flops 1048576 | bytes 4194304 | tf_op jit(solution)/shard_map/mul | solution.py:325
Async XLA Ops:
  0.6 0.7 copy-start
